TPU v7x, 512 devices: a whole 4x8x8 slice. The times are simulated.
512 devices in a mesh: blk: 8 (over x, core), pair: 64 (over z, y).
Axes of the slice: x: 4, y: 8, z: 8, core: 2. Of those that a mesh axis runs over, the one named last changes fastest.
Arguments:
- source_points: float32 [3, 524288], P(None, 'blk'), may hold values from -5 to 5
- target_points: float32 [3, 524288], P(None, 'blk'), may hold values from -5 to 5
- source_logw: float32 [524288], P('blk'), may hold values from -4 to 4
- target_logw: float32 [524288], P('blk'), may hold values from -4 to 4
- warm_start: float32 [524288], P('blk'), may hold values from -4 to 112
- pairs: int32 [8, 64, 2, 40], P('blk', 'pair'), may hold values from -1 to 2047, as said below
- owner_slot: int32 [2048], replicated, may hold values from 0 to 2047, as said below
Outputs:
- source_pot: float32 [524288], P('blk')
- target_pot: float32 [524288], P('blk')
Inputs may be any that keep to these rules, and one draw needn't show every extreme that they name: `pairs`: entry k of device (b, p) is empty (both rows -1) or live; live entries of each group of 5 positions come first, 1 to 5 of them, and some group of some device is full. A live source id s has s // 256 == b; a live target id t has owner_slot[t] // 256 == k // 5. `owner_slot`: A permutation of the storage slots.
All inputs are finite; a program needn't handle non-finite values.
Results may differ from a plain program's by a relative error of at most 0.0001.
Values sent between devices are 32-bit elements; how exact they have to be, the bound alone decides.
A program may use at most 128 MiB of HBM per device.

v0:
```python
import jax
import jax.numpy as jnp
from jax import lax
from jax.sharding import PartitionSpec as P

BS = 256
ITERS = 2


EPSILON = 0.5
DUSTBIN = 0.0
VERY_LOW = -1e30


def finish(total_max, total_sum):
    shifted = jnp.maximum(total_max, DUSTBIN)
    return -EPSILON * (
        shifted + jnp.log(jnp.exp(DUSTBIN - shifted) + total_sum * jnp.exp(total_max - shifted))
    )


def collect(onehot, index, slot_max, slot_sum):
    block_max = jnp.max(jnp.where(onehot[:, :, None], slot_max[None], VERY_LOW), axis=1)
    scaled = slot_sum * jnp.exp(slot_max - block_max[index])
    block_sum = jnp.dot(
        onehot.astype(jnp.float32),
        scaled,
        precision=lax.Precision.HIGHEST,
        preferred_element_type=jnp.float32,
    )
    return (block_max, block_sum)


def pair_combine(block_max, block_sum):
    top = lax.pmax(block_max, "pair")
    total = lax.psum(block_sum * jnp.exp(block_max - top), "pair")
    return finish(top, total)


def per_device(
    source_points, target_points, source_logw, target_logw, warm_start, pairs, owner_slot
):
    groups = lax.axis_size("blk")
    block_size = BS
    local_blocks = source_logw.shape[0] // block_size
    capacity = pairs.shape[-1] // groups
    slots = groups * capacity
    here = lax.axis_index("blk")
    src_ids = pairs[0, 0, 0]
    tgt_ids = pairs[0, 0, 1]
    live = tgt_ids >= 0
    src_local = jnp.where(live, src_ids - here * local_blocks, 0)
    storage = owner_slot[jnp.where(live, tgt_ids, 0)]
    wanted = jnp.where(live, storage % local_blocks, 0).reshape(groups, capacity)
    asked = lax.all_to_all(wanted, "blk", split_axis=0, concat_axis=0, tiled=True)
    asked_flat = asked.reshape(-1)
    block_range = jnp.arange(local_blocks, dtype=jnp.int32)[:, None]
    src_onehot = jnp.logical_and(src_local[None, :] == block_range, live[None, :])
    tgt_onehot = asked_flat[None, :] == block_range
    src_pts = source_points.reshape(3, local_blocks, block_size)[:, src_local]
    tgt_store = target_points.reshape(3, local_blocks, block_size)
    src_mass = source_logw.reshape(local_blocks, block_size)
    tgt_mass = target_logw.reshape(local_blocks, block_size)
    target_pot = warm_start.reshape(local_blocks, block_size)
    source_pot = jnp.zeros((local_blocks, block_size), jnp.float32)
    for sweep in range(ITERS):
        whole_pack = jnp.concatenate((tgt_store, tgt_mass[None], target_pot[None]), axis=0)[
            :, asked
        ]
        received = lax.all_to_all(
            whole_pack, "blk", split_axis=1, concat_axis=1, tiled=True
        ).reshape(5, slots, block_size)
        remote = received[:4]
        pot_recv = received[4]
        first = src_pts[0][:, :, None] - remote[0][:, None, :]
        second = src_pts[1][:, :, None] - remote[1][:, None, :]
        third = src_pts[2][:, :, None] - remote[2][:, None, :]
        tile = first * first + second * second + third * third
        row_term = remote[3][:, None, :] + (pot_recv[:, None, :] - tile) / EPSILON
        row_max = jnp.max(row_term, axis=2)
        row_sum = jnp.sum(jnp.exp(row_term - row_max[:, :, None]), axis=2)
        row_max = jnp.where(live[:, None], row_max, VERY_LOW)
        row_sum = jnp.where(live[:, None], row_sum, 0.0)
        block_max, block_sum = collect(src_onehot, src_local, row_max, row_sum)
        source_pot = pair_combine(block_max, block_sum)
        col_term = (
            src_mass[src_local][:, :, None] + (source_pot[src_local][:, :, None] - tile) / EPSILON
        )
        col_max = jnp.max(col_term, axis=1)
        col_sum = jnp.sum(jnp.exp(col_term - col_max[:, None, :]), axis=1)
        col_max = jnp.where(live[:, None], col_max, VERY_LOW)
        col_sum = jnp.where(live[:, None], col_sum, 0.0)
        back_max, back_sum = (
            lax.all_to_all(
                col_max.reshape(groups, capacity, block_size),
                "blk",
                split_axis=0,
                concat_axis=0,
                tiled=True,
            ),
            lax.all_to_all(
                col_sum.reshape(groups, capacity, block_size),
                "blk",
                split_axis=0,
                concat_axis=0,
                tiled=True,
            ),
        )
        block_max, block_sum = collect(
            tgt_onehot,
            asked_flat,
            back_max.reshape(slots, block_size),
            back_sum.reshape(slots, block_size),
        )
        target_pot = pair_combine(block_max, block_sum)
    return (source_pot.reshape(-1), target_pot.reshape(-1))


def solution(mesh):
    return jax.shard_map(
        per_device,
        mesh=mesh,
        in_specs=(
            P(None, "blk"),
            P(None, "blk"),
            P("blk"),
            P("blk"),
            P("blk"),
            P("blk", "pair", None, None),
            P(),
        ),
        out_specs=(P("blk"), P("blk")),
        check_vma=False,
    )
```

profile of v0, /device:TPU:6, one launch (start us, length us, event | category | flops | bytes accessed | tf_op | source)
XLA Modules:
  0.0 1359.0 jit_solution(14044118933644455092)
XLA Ops:
  7.2 1.3 compare_bitcast_fusion
  9.3 1.5 gather_fusion
  11.5 9.1 all-to-all-start
  20.6 1.3 bitcast_select_fusion
  22.7 2.1 pad_maximum_fusion
  28.1 4.8 all-to-all-start.1
  33.5 5.5 all-to-all-done.1
  39.2 6.7 fusion
  46.0 4.3 select_reduce_fusion.3
  50.4 9.3 exponential_reduce_fusion.3
  60.3 142.3 %all-reduce.9.cloned.1.call-done = f32[256,256]{1,0:T(8,128)} async-done(((f32[256,256]{1,0:T(8,128)}), f32[256,256]{1,0:T(8,128)}) %all-reduce.9.cloned.1.call-update) | async-done | bytes 262160 | tf_op jit(solution)/shard_map/pmax | solution.py:35
  202.6 2.1 convolution_multiply_fusion.3
  206.8 148.3 %all-reduce.11.cloned.1.call-done = f32[256,256]{1,0:T(8,128)} async-done(((f32[256,256]{1,0:T(8,128)}), f32[256,256]{1,0:T(8,128)}) %all-reduce.11.cloned.1.call-update) | async-done | bytes 262160 | tf_op jit(solution)/shard_map/psum | solution.py:36
  355.1 1.1 fusion.9
  356.8 8.4 fusion.1
  365.3 8.7 exponential_reduce_fusion.2
  374.8 4.8 all-to-all-start.2
  379.7 3.4 all-to-all-done.2
  383.1 4.3 select_reduce_fusion.2
  387.5 5.4 all-to-all-start.3
  392.8 1.6 gather_fusion.6
  394.4 1.9 all-to-all-done.3
  396.4 139.5 %all-reduce.13.cloned.1.call-done = f32[256,256]{1,0:T(8,128)} async-done(((f32[256,256]{1,0:T(8,128)}), f32[256,256]{1,0:T(8,128)}) %all-reduce.13.cloned.1.call-update) | async-done | bytes 262160 | tf_op jit(solution)/shard_map/pmax | solution.py:35
  535.9 2.0 convolution_multiply_fusion.2
  538.0 150.4 %all-reduce.15.cloned.1.call-done = f32[256,256]{1,0:T(8,128)} async-done(((f32[256,256]{1,0:T(8,128)}), f32[256,256]{1,0:T(8,128)}) %all-reduce.15.cloned.1.call-update) | async-done | bytes 262160 | tf_op jit(solution)/shard_map/psum | solution.py:36
  688.3 1.2 fusion.16
  689.8 2.0 pad_maximum_fusion.1
  691.8 2.2 gather_fusion.7
  694.1 10.8 all_to_all.39
  705.0 6.7 fusion.2
  711.8 4.3 select_reduce_fusion.1
  716.1 9.3 exponential_reduce_fusion.1
  726.0 138.5 %all-reduce.17.cloned.1.call-done = f32[256,256]{1,0:T(8,128)} async-done(((f32[256,256]{1,0:T(8,128)}), f32[256,256]{1,0:T(8,128)}) %all-reduce.17.cloned.1.call-update) | async-done | bytes 262160 | tf_op jit(solution)/shard_map/pmax | solution.py:35
  864.5 2.0 convolution_multiply_fusion.1
  866.8 150.2 %all-reduce.19.cloned.1.call-done = f32[256,256]{1,0:T(8,128)} async-done(((f32[256,256]{1,0:T(8,128)}), f32[256,256]{1,0:T(8,128)}) %all-reduce.19.cloned.1.call-update) | async-done | bytes 262160 | tf_op jit(solution)/shard_map/psum | solution.py:36
  1017.0 1.2 fusion.22
  1018.7 8.4 fusion.3
  1027.2 8.7 exponential_reduce_fusion
  1036.7 8.1 all_to_all.40
  1044.8 4.3 select_reduce_fusion
  1049.1 5.4 all-to-all-start.6
  1054.5 1.6 gather_fusion.10
  1056.1 2.0 all-to-all-done.6
  1058.0 139.5 %all-reduce.21.cloned.1.call-done = f32[256,256]{1,0:T(8,128)} async-done(((f32[256,256]{1,0:T(8,128)}), f32[256,256]{1,0:T(8,128)}) %all-reduce.21.cloned.1.call-update) | async-done | bytes 262160 | tf_op jit(solution)/shard_map/pmax | solution.py:35
  1197.6 2.0 convolution_multiply_fusion
  1199.6 0.8 copy.39
  1200.4 149.7 %all-reduce.23.cloned.1.call-done = f32[256,256]{1,0:T(8,128)} async-done(((f32[256,256]{1,0:T(8,128)}), f32[256,256]{1,0:T(8,128)}) %all-reduce.23.cloned.1.call-update) | async-done | bytes 262160 | tf_op jit(solution)/shard_map/psum | solution.py:36
  1350.1 1.2 fusion.29
  (106 shorter events, 14.5 us)
Async XLA Ops:
  7.2 14.7 %copy-start = (f32[3,65536]{1,0:T(4,128)S(1)}, f32[3,65536]{1,0:T(4,128)}, u32[]{:S(2)}) copy-start(f32[3,65536]{1,0:T(4,128)} %param.7) | copy-start | bytes 2359300
  11.5 13.8 %all-to-all-start = ((s32[8,1,5]{2,1,0:T(1,128)}), s32[8,1,5]{2,1,0:T(1,128)S(1)}, u32[]{:S(2)}, u32[]{:S(2)}) async-start(s32[8,1,5]{2,1,0:T(1,128)} %bitcast.6), calls=%async_computation | async-start | bytes 8192 | tf_op jit(solution)/shard_map/all_to_all | solution.py:55
  21.9 0.7 copy-start.12
  25.4 0.6 copy-start.8
  27.3 11.9 copy-start.6
  27.3 18.6 %copy-start.11 = (pred[40]{0:T(512)(128)(4,1)S(1)}, pred[40]{0:T(512)(128)(4,1)}, u32[]{:S(2)}) copy-start(pred[40]{0:T(512)(128)(4,1)} %get-tuple-element.19) | copy-start | bytes 124
  28.1 11.0 all-to-all-start.1
  32.9 169.7 %all-reduce.9.cloned.1.call-start = ((), (), s32[]{:S(2)}) async-start(), calls=%async_computation.7 | async-start | bytes 524288 | tf_op jit(solution)/shard_map/pmax | solution.py:35
  50.3 9.4 copy-start.2
  50.3 9.4 copy-start.13
  50.3 152.2 %copy-start.14 = (s32[40]{0:T(128)S(1)}, s32[40]{0:T(128)}, u32[]{:S(2)}) copy-start(s32[40]{0:T(128)} %bitcast_select_fusion) | copy-start | bytes 484
  50.3 154.4 %copy-start.7 = (f32[65536]{0:T(1024)S(1)}, f32[65536]{0:T(1024)}, u32[]{:S(2)}) copy-start(f32[65536]{0:T(1024)} %param.9) | copy-start | bytes 786436
  50.3 304.8 %all-reduce.11.cloned.1.call-start = ((), (), s32[]{:S(2)}) async-start(), calls=%async_computation.8 | async-start | bytes 524288 | tf_op jit(solution)/shard_map/psum | solution.py:36
  59.7 146.4 %copy-start.9 = (s32[8,1,5]{2,1,0:T(1,128)S(1)}, s32[8,1,5]{2,1,0:T(1,128)}, u32[]{:S(2)}) copy-start(s32[8,1,5]{2,1,0:T(1,128)} %copy-done.8) | copy-start | bytes 484
  202.6 152.6 %copy-start.5 = (f32[256,256]{1,0:T(8,128)S(1)}, f32[256,256]{1,0:T(8,128)}, u32[]{:S(2)}) copy-start(f32[256,256]{1,0:T(8,128)} %all-reduce.9.cloned.1.call-done) | copy-start | bytes 786436
  374.0 315.8 %copy-start.3 = (f32[3,65536]{1,0:T(4,128)S(1)}, f32[3,65536]{1,0:T(4,128)}, u32[]{:S(2)}) copy-start(f32[3,65536]{1,0:T(4,128)} %param.8) | copy-start | bytes 2359300
  374.0 315.8 %copy-start.4 = (f32[65536]{0:T(1024)S(1)}, f32[65536]{0:T(1024)}, u32[]{:S(2)}) copy-start(f32[65536]{0:T(1024)} %param.10) | copy-start | bytes 786436
  374.8 8.4 all-to-all-start.2
  379.6 156.3 %all-reduce.13.cloned.1.call-start = ((), (), s32[]{:S(2)}) async-start(), calls=%async_computation.9 | async-start | bytes 524288 | tf_op jit(solution)/shard_map/pmax | solution.py:35
  387.5 8.9 all-to-all-start.3
  392.8 295.5 %all-reduce.15.cloned.1.call-start = ((), (), s32[]{:S(2)}) async-start(), calls=%async_computation.10 | async-start | bytes 524288 | tf_op jit(solution)/shard_map/psum | solution.py:36
  537.9 326.6 %all-reduce.17.cloned.1.call-start = ((), (), s32[]{:S(2)}) async-start(), calls=%async_computation.11 | async-start | bytes 524288 | tf_op jit(solution)/shard_map/pmax | solution.py:35
  689.5 2.3 copy-start.10
  716.1 9.3 copy-start.1
  716.1 300.9 %all-reduce.19.cloned.1.call-start = ((), (), s32[]{:S(2)}) async-start(), calls=%async_computation.12 | async-start | bytes 524288 | tf_op jit(solution)/shard_map/psum | solution.py:36
  866.5 331.0 %all-reduce.21.cloned.1.call-start = ((), (), s32[]{:S(2)}) async-start(), calls=%async_computation.13 | async-start | bytes 524288 | tf_op jit(solution)/shard_map/pmax | solution.py:35
  1049.1 8.9 all-to-all-start.6
  1054.5 295.6 %all-reduce.23.cloned.1.call-start = ((), (), s32[]{:S(2)}) async-start(), calls=%async_computation.14 | async-start | bytes 524288 | tf_op jit(solution)/shard_map/psum | solution.py:36
Sparse Core Ops, SparseCore 0:
  50.4 152.0 all-reduce.8
  206.7 148.4 all-reduce.10
  387.6 148.2 all-reduce.12
  539.9 148.4 all-reduce.14
  716.2 148.2 all-reduce.16
  868.5 148.4 all-reduce.18
  1049.2 148.2 all-reduce.20
  1201.7 148.4 all-reduce.22
where the time goes:
time: 1360 us
  waiting for transfers between devices  1170 us (86%)
  other arithmetic  99.5 us (7%)
  starting transfers between devices  29.8 us (2%)
  blocking collectives  18.9 us (1%)
  local copies, waits for them, and re-layouts  16.7 us (1%)
  between operations  14.6 us (1%)
    psum x4, waiting for transfers between devices, pair_combine(): total = lax.psum(block_sum * jnp.exp(block_max - top), 'pair')  599 us
    pmax x4, waiting for transfers between devices, pair_combine(): top = lax.pmax(block_max, 'pair')  560 us
  transfers between devices with their start and end apart: 13, of which 12 were waited for; matrix products, arithmetic and copies ran while one was open for 2% of the time, Pallas kernels for 0%

commit v1 on v0

v1 whole, which is shorter than its diff:
```python
import functools

import jax
import jax.numpy as jnp
from jax import lax
from jax.experimental import pallas as pl
from jax.experimental.pallas import tpu as pltpu
from jax.sharding import PartitionSpec as P

BS = 256
ITERS = 2
GROUP_ROWS = 8
LOG2E = 1.4426950408889634
LN2 = 0.6931471805599453
EPSILON = 0.5
INV_EPS2 = LOG2E / EPSILON
LOW = -1e30
MESH = pl.DeviceIdType.MESH
F32 = jnp.float32


def log2(value):
    return jnp.log(value) * LOG2E


def split3(value):
    high = value.astype(jnp.bfloat16).astype(F32)
    rest = value - high
    middle = rest.astype(jnp.bfloat16).astype(F32)
    return high, middle, rest - middle


def tile_terms(rows, columns):
    r1, r2, r3 = split3(rows)
    c1, c2, c3 = split3(columns)
    left = jnp.concatenate((r1, r1, r2, r2, r1, r3), axis=0).astype(jnp.bfloat16)
    right = jnp.concatenate((c1, c2, c1, c2, c3, c1), axis=0).astype(jnp.bfloat16)
    return lax.dot_general(left, right, (((0,), (0,)), ((), ())), preferred_element_type=F32)


def lse_rows(terms):
    top = jnp.max(terms, axis=0, keepdims=True)
    return top + log2(jnp.sum(jnp.exp2(terms - top), axis=0, keepdims=True))


def wait_bytes(ref, sem):
    pltpu.make_async_copy(ref, ref, sem).wait()


def gather(hot, table):
    total = None
    for part in split3(table):
        one = jnp.dot(hot, part.astype(jnp.bfloat16), preferred_element_type=F32)
        total = one if total is None else total + one
    return total


def kernel(
    groups, side, capacity, nb,
    pairs_v, owner, src_pts, tgt_pts, src_mass, tgt_mass, warm,
    out_src, out_tgt,
    ids_send, ids_src, ids_tgt, hot_src, hot_tgt, pick_src, pick_tgt,
    got, src_pack, send_pack, recv_pack, mass_src, mass_tgt, bias_src, send_pot, recv_pot,
    terms, merged, send_col, recv_col, dense, stage1, stage2, full,
    ids_sem, pack_sem, pot_sem, col_sem, red_sem,
):
    b = lax.axis_index("blk")
    p = lax.axis_index("pair")
    z, y = p // side, p % side
    rows = groups * GROUP_ROWS
    seg = nb // 2 // side

    def blk_peer(d):
        return {"blk": lax.rem(b + d, groups)}

    def y_peer(d):
        return {"pair": z * side + lax.rem(y + d, side)}

    def z_peer(d):
        return {"pair": lax.rem(z + d, side) * side + y}

    barrier = pltpu.get_barrier_semaphore()

    def greet(peer, count):
        def one(d, carry):
            pl.semaphore_signal(barrier, inc=1, device_id=peer(d), device_id_type=MESH)
            return carry

        lax.fori_loop(1, count, one, 0)

    greet(blk_peer, groups)
    greet(y_peer, side)
    greet(z_peer, side)

    def send_all(peer, count, src_of, dst, sems):
        def one(d, carry):
            pltpu.make_async_remote_copy(
                src_ref=src_of(d), dst_ref=dst, send_sem=sems.at[0], recv_sem=sems.at[1],
                device_id=peer(d), device_id_type=MESH,
            ).start()
            return carry

        lax.fori_loop(1, count, one, 0)

    row = lax.broadcasted_iota(jnp.int32, (rows, 128), 0)
    lane = lax.broadcasted_iota(jnp.int32, (rows, 128), 1)
    group, member = row // GROUP_ROWS, row % GROUP_ROWS
    listed = member < capacity
    own_lane = jnp.where(listed, group * capacity + member, -1) == lane

    def column(values):
        return jnp.sum(jnp.where(own_lane, values.astype(F32), 0.0), axis=1, keepdims=True)

    source_id = jnp.broadcast_to(column(pairs_v[0:1, :]), (rows, 128)).astype(jnp.int32)
    target_id = jnp.broadcast_to(column(pairs_v[1:2, :]), (rows, 128)).astype(jnp.int32)
    live = listed & (target_id >= 0)
    ids_src[...] = jnp.where(live, source_id - b * nb, -1).reshape(groups, GROUP_ROWS, 128)
    table_rows = owner.shape[0]
    high = jnp.where(target_id[:, :table_rows] // 128 == lane[:, :table_rows], 1.0, 0.0)
    slot = gather(high.astype(jnp.bfloat16), owner[...].astype(F32))
    slot = jnp.sum(jnp.where(target_id % 128 == lane, slot, 0.0), axis=1, keepdims=True)
    slot = jnp.broadcast_to(slot, (rows, 128)).astype(jnp.int32)
    ids_send[...] = jnp.where(live, slot - group * nb, -1).reshape(groups, GROUP_ROWS, 128)

    pl.semaphore_wait(barrier, groups - 1 + 2 * (side - 1))
    send_all(blk_peer, groups, lambda d: ids_send.at[lax.rem(b + d, groups)], ids_tgt.at[b], ids_sem)
    ids_tgt[b] = ids_send[b]

    row8 = lax.broadcasted_iota(jnp.int32, (GROUP_ROWS, BS), 0)
    low_rows = jnp.full((groups, GROUP_ROWS, BS), LOW, F32)
    terms[...] = low_rows
    merged[...] = low_rows
    for it in range(ITERS):
        send_col[it] = low_rows

    def one_hots(ids, place, pick):
        ids = ids[...].reshape(rows, 128)
        if nb > 128:
            wide = jnp.concatenate([ids] * (nb // 128), axis=1)
        else:
            wide = ids[:, :nb]
        match = wide == lax.broadcasted_iota(jnp.int32, (rows, nb), 1)
        pick[...] = jnp.where(match, 1.0, 0.0).astype(jnp.bfloat16)
        lanes = jnp.sum(jnp.where(row == lane, ids.astype(F32), 0.0), axis=0, keepdims=True)
        again = jnp.where((ids.astype(F32) == lanes) & (row < lane), 1.0, 0.0)
        again = jnp.max(again, axis=0, keepdims=True)
        block = lax.broadcasted_iota(jnp.int32, (nb, 128), 0).astype(F32)
        lane_nb = lax.broadcasted_iota(jnp.int32, (nb, 128), 1)
        first = jnp.where((lane_nb < rows) & (again == 0.0) & (block == lanes), 1.0, 0.0)
        none = jnp.where(jnp.sum(first, axis=1, keepdims=True) > 0.0, 0.0, 1.0)
        place[...] = jnp.where(lane_nb == rows, none, first).astype(jnp.bfloat16)

    def make_pack(pack, places, ones):
        fixed = jnp.zeros((GROUP_ROWS, BS), F32)
        for r in ones:
            fixed = jnp.where(row8 == r, 1.0, fixed)

        def one_group(g, carry):
            for c in range(capacity):
                k = g * capacity + c
                pack[k] = fixed
                for i, r in enumerate(places):
                    pack[k, r : r + 1, :] = got[i, g, c : c + 1, :]
            return carry

        lax.fori_loop(0, groups, one_group, 0)

    def fetch_points(pick, points, scale):
        square = None
        for i in range(3):
            x = gather(pick[...], points[i])
            got[i] = (x * scale).reshape(groups, GROUP_ROWS, BS)
            square = x * x if square is None else square + x * x
        got[3] = (square * (-INV_EPS2)).reshape(groups, GROUP_ROWS, BS)

    shape3 = (groups, GROUP_ROWS, BS)
    one_hots(ids_src, hot_src, pick_src)
    fetch_points(pick_src, src_pts, 2.0 * INV_EPS2)
    make_pack(src_pack, (0, 1, 2, 4), (3, 5))
    mass_src[...] = (gather(pick_src[...], src_mass[...]) * LOG2E).reshape(shape3)

    wait_bytes(ids_tgt.at[pl.ds(0, groups - 1)], ids_sem.at[1])
    one_hots(ids_tgt, hot_tgt, pick_tgt)
    fetch_points(pick_tgt, tgt_pts, 1.0)
    mass = gather(pick_tgt[...], tgt_mass[...]) * LOG2E
    mass_tgt[...] = mass.reshape(shape3)
    got[4] = (mass + gather(pick_tgt[...], warm[...]) * INV_EPS2).reshape(shape3)
    make_pack(send_pack, (0, 1, 2, 3, 5), (4,))

    def block_of(g):
        return pl.ds(g * capacity, capacity)

    send_all(
        blk_peer, groups, lambda d: send_pack.at[block_of(lax.rem(b + d, groups))],
        recv_pack.at[block_of(b)], pack_sem,
    )
    for c in range(capacity):
        recv_pack[b * capacity + c] = send_pack[b * capacity + c]
    wait_bytes(recv_pack.at[pl.ds(0, (groups - 1) * capacity)], pack_sem.at[1])

    def merge_and_place(ids, values, hot, target):
        def one_group(g, carry):
            for c in range(capacity):
                same = ids[...].reshape(rows, 128) == ids[g, c : c + 1, :]
                for h in range(BS // 128):
                    part = values[:, :, 128 * h : 128 * (h + 1)].reshape(rows, 128)
                    picked = jnp.where(same, part, LOW)
                    merged[g, c : c + 1, 128 * h : 128 * (h + 1)] = lse_rows(picked)
            return carry

        lax.fori_loop(0, groups, one_group, 0)
        one, two, three = split3(merged[...].reshape(rows, BS))
        last = 128 - rows
        none = jnp.full((last, BS), LOW, F32)
        zero = jnp.zeros((last, BS), F32)
        first = jnp.concatenate((one, none), axis=0).astype(jnp.bfloat16)
        total = jnp.dot(hot[...], first, preferred_element_type=F32)
        for part in (two, three):
            more = jnp.concatenate((part, zero), axis=0).astype(jnp.bfloat16)
            total = total + jnp.dot(hot[...], more, preferred_element_type=F32)
        target[...] = total

    def reduce_pairs(a):
        places = (y, z)
        firsts = (y_peer, z_peer)
        seconds = (z_peer, y_peer)
        for h in range(2):
            mine = places[h]

            def chunk(d, h=h, mine=mine):
                first = h * (nb // 2) + lax.rem(mine + d, side) * seg
                return dense.at[a, pl.ds(pl.multiple_of(first, seg), seg)]

            send_all(firsts[h], side, chunk, stage1.at[a, h, mine], red_sem.at[a, h, 0])
            own = pl.multiple_of(h * (nb // 2) + mine * seg, seg)
            stage1[a, h, mine] = dense[a, pl.ds(own, seg), :]
        for h in range(2):
            wait_bytes(stage1.at[a, h, pl.ds(0, side - 1)], red_sem.at[a, h, 0, 1])
            arrived = stage1[a, h]
            top = jnp.max(arrived, axis=0)
            part = top + log2(jnp.sum(jnp.exp2(arrived - top[None]), axis=0))
            other = places[1 - h]
            stage2[a, h, other] = part
            send_all(
                seconds[h], side, lambda d, h=h, other=other: stage2.at[a, h, other],
                stage2.at[a, h, other], red_sem.at[a, h, 1],
            )
        for h in range(2):
            mine = places[h]
            wait_bytes(stage2.at[a, h, pl.ds(0, side - 1)], red_sem.at[a, h, 1, 1])
            arrived = stage2[a, h]
            top = jnp.maximum(jnp.max(arrived, axis=0), 0.0)
            total = jnp.exp2(-top) + jnp.sum(jnp.exp2(arrived - top[None]), axis=0)
            own = pl.multiple_of(h * (nb // 2) + mine * seg, seg)
            full[a, pl.ds(own, seg), :] = top + log2(total)
            place = full.at[a, pl.ds(own, seg)]
            send_all(firsts[h], side, lambda d, place=place: place, place, red_sem.at[a, h, 2])
        for h in range(2):
            wait_bytes(full.at[a, pl.ds(0, (side - 1) * seg)], red_sem.at[a, h, 2, 1])

    for it in range(ITERS):
        if it > 0:
            pot = gather(pick_tgt[...], full[2 * it - 1])
            send_pot[...] = mass_tgt[...] - pot.reshape(shape3)
            send_all(
                blk_peer, groups, lambda d: send_pot.at[lax.rem(b + d, groups)],
                recv_pot.at[b], pot_sem,
            )
            recv_pot[b] = send_pot[b]
            wait_bytes(recv_pot.at[pl.ds(0, groups - 1)], pot_sem.at[1])

        def row_group(g, carry, it=it):
            for c in range(capacity):
                k = g * capacity + c
                target = recv_pack[k]
                if it > 0:
                    target = jnp.where(row8 == 5, recv_pot[g, c : c + 1, :], target)
                terms[g, c : c + 1, :] = lse_rows(tile_terms(target, src_pack[k]))
            return carry

        lax.fori_loop(0, groups, row_group, 0)
        merge_and_place(ids_src, terms, hot_src, dense.at[2 * it])
        reduce_pairs(2 * it)

        bias_src[...] = mass_src[...] - gather(pick_src[...], full[2 * it]).reshape(shape3)

        def column_group(g, carry, it=it):
            for c in range(capacity):
                k = g * capacity + c
                source = jnp.where(row8 == 5, bias_src[g, c : c + 1, :], src_pack[k])
                target = jnp.where(row8 == 5, 1.0, recv_pack[k])
                send_col[it, g, c : c + 1, :] = lse_rows(tile_terms(source, target))
            return carry

        lax.fori_loop(0, groups, column_group, 0)
        send_all(
            blk_peer, groups, lambda d, it=it: send_col.at[it, lax.rem(b + d, groups)],
            recv_col.at[it, b], col_sem.at[it],
        )
        recv_col[it, b] = send_col[it, b]
        wait_bytes(recv_col.at[it, pl.ds(0, groups - 1)], col_sem.at[it, 1])
        terms[...] = recv_col[it]
        merge_and_place(ids_tgt, terms, hot_tgt, dense.at[2 * it + 1])
        reduce_pairs(2 * it + 1)

    out_src[...] = full[2 * ITERS - 2] * (-EPSILON * LN2)
    out_tgt[...] = full[2 * ITERS - 1] * (-EPSILON * LN2)

    def drain(sem, ref, count):
        def one(d, carry):
            wait_bytes(ref, sem)
            return carry

        lax.fori_loop(1, count, one, 0)

    drain(ids_sem.at[0], ids_send.at[0], groups)
    drain(pack_sem.at[0], send_pack.at[pl.ds(0, capacity)], groups)
    if ITERS > 1:
        drain(pot_sem.at[0], send_pot.at[0], groups)
    for it in range(ITERS):
        drain(col_sem.at[it, 0], send_col.at[it, 0], groups)
    for a in range(2 * ITERS):
        for h in range(2):
            for stage in range(3):
                drain(red_sem.at[a, h, stage, 0], dense.at[a, pl.ds(0, seg)], side)


def per_device(
    source_points, target_points, source_logw, target_logw, warm_start, pairs, owner_slot
):
    groups = lax.axis_size("blk")
    side = round(lax.axis_size("pair") ** 0.5)
    points = source_logw.shape[0]
    nb = points // BS
    capacity = pairs.shape[-1] // groups
    entries = groups * capacity
    rows = groups * GROUP_ROWS
    seg = nb // 2 // side
    reductions = 2 * ITERS
    pairs = pairs[0, 0]
    padded = jnp.pad(pairs, ((0, 6), (0, 128 - entries)), constant_values=-1)
    slots = -(-owner_slot.shape[0] // 2048) * 2048
    owner = jnp.pad(owner_slot, (0, slots - owner_slot.shape[0])).reshape(-1, 128)
    vmem = pl.BlockSpec(memory_space=pltpu.VMEM)
    out = jax.ShapeDtypeStruct((nb, BS), F32)
    dma = pltpu.SemaphoreType.DMA
    source_pot, target_pot = pl.pallas_call(
        functools.partial(kernel, groups, side, capacity, nb),
        out_shape=(out, out),
        in_specs=[vmem] * 7,
        out_specs=(vmem, vmem),
        scratch_shapes=[
            *[pltpu.VMEM((groups, GROUP_ROWS, 128), jnp.int32)] * 3,
            *[pltpu.VMEM((nb, 128), jnp.bfloat16)] * 2,
            *[pltpu.VMEM((rows, nb), jnp.bfloat16)] * 2,
            pltpu.VMEM((5, groups, GROUP_ROWS, BS), F32),
            *[pltpu.VMEM((entries, GROUP_ROWS, BS), F32)] * 3,
            *[pltpu.VMEM((groups, GROUP_ROWS, BS), F32)] * 7,
            *[pltpu.VMEM((ITERS, groups, GROUP_ROWS, BS), F32)] * 2,
            pltpu.VMEM((reductions, nb, BS), F32),
            *[pltpu.VMEM((reductions, 2, side, seg, BS), F32)] * 2,
            pltpu.VMEM((reductions, nb, BS), F32),
            dma((2,)),
            dma((2,)),
            dma((2,)),
            dma((ITERS, 2)),
            dma((reductions, 2, 3, 2)),
        ],
        compiler_params=pltpu.CompilerParams(
            collective_id=0, has_side_effects=True, vmem_limit_bytes=40 * 1024 * 1024
        ),
        name="sinkhorn",
    )(
        padded, owner,
        source_points.reshape(3, nb, BS), target_points.reshape(3, nb, BS),
        source_logw.reshape(nb, BS), target_logw.reshape(nb, BS), warm_start.reshape(nb, BS),
    )
    return source_pot.reshape(-1), target_pot.reshape(-1)


def solution(mesh):
    return jax.shard_map(
        per_device,
        mesh=mesh,
        in_specs=(
            P(None, "blk"),
            P(None, "blk"),
            P("blk"),
            P("blk"),
            P("blk"),
            P("blk", "pair", None, None),
            P(),
        ),
        out_specs=(P("blk"), P("blk")),
        check_vma=False,
    )
```

time: 1360 us -> 140 us (0.10)
  waiting for transfers between devices: 1170 us -> 0 us
  Pallas kernels: 0 us -> 131 us
  other arithmetic: 99.5 us -> 0 us
  starting transfers between devices: 29.8 us -> 0 us
  blocking collectives: 18.9 us -> 0 us
  between operations: 14.6 us -> 0.68 us
    psum x4 -> x0, waiting for transfers between devices: 599 us -> none  [pair_combine(): total = lax.psum(block_sum * jnp.exp(block_max - top), 'pair')]
    pmax x4 -> x0, waiting for transfers between devices: 560 us -> none  [pair_combine(): top = lax.pmax(block_max, 'pair')]
    pallas_call x0 -> x1, Pallas kernels: none -> 131 us  [per_device(): pl.pallas_call(functools.partial(kernel, groups, side, capacity, nb), out...]
    reduce_max x8 -> x0, other arithmetic: 47.4 us -> none  [the longest x4 17.1 us: collect(): jnp.max(jnp.where(onehot[:, :, None], slot_max[None], VERY_LOW), axis=1)]
    reduce_sum x4 -> x0, other arithmetic: 35.9 us -> none  [the longest x2 18.5 us: per_device(): row_sum = jnp.sum(jnp.exp(row_term - row_max[:, :, None]), axis=2)]
    all_to_all x5 -> x0, starting transfers between devices: 29.4 us -> none  [the longest x2 10.7 us: per_device(): lax.all_to_all(col_sum.reshape(groups, capacity, block_size), 'blk', spli...]
    all_to_all x2 -> x0, blocking collectives: 18.9 us -> none  [the longest x1 10.8 us: per_device(): lax.all_to_all(whole_pack, 'blk', split_axis=1, concat_axis=1, tiled=True)]
  transfers between devices with their start and end apart: 13 -> 0, of which waited for: 12 -> 0; matrix products, arithmetic and copies ran while one was open for 2% -> 0% of each run, Pallas kernels for 0% -> 0%
where the time goes in v1:
time: 140 us; the launch traced here: 138 us
  Pallas kernels  131 us (94%)
  local copies, waits for them, and re-layouts  7.09 us (5%)
    pallas_call x1, Pallas kernels, per_device(): pl.pallas_call(functools.partial(kernel, groups, side, capacity, nb), out...  131 us

profile of v1, /device:TPU:6, one launch (start us, length us, event | category | flops | bytes accessed | tf_op | source)
XLA Modules:
  0.0 138.4 jit_solution(6059788442659922424)
XLA Ops:
  0.6 0.0 copy-start.1
  0.6 0.8 pad.4.pairs_v
  1.4 1.0 reshape.31.src_mass
  2.4 1.0 reshape.32.tgt_mass
  3.5 1.0 reshape.33.warm
  4.5 0.0 copy-done.1
  4.5 0.0 copy-start
  4.5 1.5 %copy_bitcast_fusion = (f32[3,256,256]{2,1,0:T(8,128)S(1)}, f32[3,256,256]{2,1,0:T(8,128)S(1)}) fusion(f32[1,3,256,256]{3,1,2,0:T(4,128)S(1)} %bitcast.15, f32[1,3,256,256]{3,1,2,0:T(4,128)} %bitcast.16), kind=kLoop, calls=%fused_computation | loop fusion | bytes 3145728 | tf_op jit(solution)/shard_map/reshape | solution.py:375
  6.1 0.0 copy-done
  6.1 130.6 %sinkhorn.1 = (f32[256,256]{1,0:T(8,128)S(1)}, f32[256,256]{1,0:T(8,128)S(1)}) custom-call(s32[8,128]{1,0:T(8,128)S(1)} %pad.4.pairs_v, s32[16,128]{1,0:T(8,128)S(1)} %bitcast.14, f32[3,256,256]{2,1,0:T(8,128)S(1)} %get-tuple-element.7.src_pts, f32[3,256,256]{2,1,0:T(8,128)S(1)} %get-tuple-element.6.tgt_pts, f32[256,256]{1,0:T(8,128)S(1)} %reshape.31.src_mass, ...), custom_call_target="tpu_custom_call" | custom-call | tf_op jit(solution)/shard_map/sinkhorn/pallas_call | solution.py:347
  136.7 0.8 copy.11
  137.5 0.8 copy.12
Async XLA Ops:
  0.6 3.9 %copy-start.1 = (f32[3,65536]{1,0:T(4,128)S(1)}, f32[3,65536]{1,0:T(4,128)}, u32[]{:S(2)}) copy-start(f32[3,65536]{1,0:T(4,128)} %param.8) | copy-start | bytes 2359300
  4.5 1.6 %copy-start = (s32[2048]{0:T(1024)S(1)}, s32[2048]{0:T(1024)}, u32[]{:S(2)}) copy-start(s32[2048]{0:T(1024)} %param.13) | copy-start | bytes 24580

commit v2 on v0

v2 whole, which is shorter than its diff:
```python
import functools

import jax
import jax.numpy as jnp
from jax import lax
from jax.experimental import pallas as pl
from jax.experimental.pallas import tpu as pltpu
from jax.sharding import PartitionSpec as P

BS = 256
HALF = 128
ITERS = 2
GROUP_ROWS = 8
LOG2E = 1.4426950408889634
LN2 = 0.6931471805599453
EPSILON = 0.5
INV_EPS2 = LOG2E / EPSILON
LOW = -1e30
MESH = pl.DeviceIdType.MESH
F32 = jnp.float32
BF16 = jnp.bfloat16


def log2(value):
    return jnp.log(value) * LOG2E


def split3(value):
    high = value.astype(BF16).astype(F32)
    rest = value - high
    middle = rest.astype(BF16).astype(F32)
    return high, middle, rest - middle


def left_parts(value):
    one, two, three = split3(value)
    return jnp.concatenate((one, one, two, two, one, three), axis=0).astype(BF16)


def right_parts(value):
    one, two, three = split3(value)
    return jnp.concatenate((one, two, one, two, three, one), axis=0).astype(BF16)


def tile_lse(left, right):
    terms = lax.dot_general(left, right, (((0,), (0,)), ((), ())), preferred_element_type=F32)
    top = jnp.max(terms, axis=0, keepdims=True)
    return top + log2(jnp.sum(jnp.exp2(terms - top), axis=0, keepdims=True))


def lse_pair(first, second):
    top = jnp.maximum(first, second)
    return top + log2(jnp.exp2(first - top) + jnp.exp2(second - top))


def tile_all(lefts, rights):
    return [tile_lse(one, two) for one, two in zip(lefts, rights)]


def gather(hot, parts):
    total = None
    for part in parts:
        one = jnp.dot(hot, part.astype(BF16), preferred_element_type=F32)
        total = one if total is None else total + one
    return total


def lanes_of(h):
    return slice(h * HALF, (h + 1) * HALF)


def wait_bytes(ref, sem):
    pltpu.make_async_copy(ref, ref, sem).wait()


def far_first(k, size):
    return size // 2 + (1 - 2 * (k % 2)) * ((k + 1) // 2)


def kernel(
    groups, side, capacity, nb,
    pairs_v, owner, src_pts, tgt_pts, src_mass, tgt_mass, warm,
    out_src, out_tgt,
    ids_send, ids_src, ids_tgt, own_ids, lists, place, pick, pick_src, pick_tgt, table,
    got_src, got_send, got_recv, src_pack, tgt_pack, left, right_src, right_tgt,
    mass_src, mass_tgt, bias, send_pot, recv_pot, terms, partial, values_c, merged, send_col, recv_col,
    spread, spread_got, placed, row_sum, asked, asked_got, dense, stage1, stage2, full,
    ids_sem, list_sem, pack_sent, pack_sem, pot_sent, pot_sem, col_sem, spread_sem, red_sem,
):
    b = lax.axis_index("blk")
    p = lax.axis_index("pair")
    z, y = p // side, p % side
    rows = groups * GROUP_ROWS
    seg = nb // side
    chips = groups // 2

    def blk_index(k):
        x = lax.rem(b // 2 + far_first(k // 2, chips), chips)
        return x * 2 + lax.rem(b + 1 + k, 2)

    def near(k):
        return blk_index(groups - 1 - k)

    def y_index(k):
        return z * side + lax.rem(y + far_first(k, side), side)

    def z_index(k):
        return lax.rem(z + far_first(k, side), side) * side + y

    barrier = pltpu.get_barrier_semaphore()

    def greet(axis, index, count):
        def one(k, carry):
            pl.semaphore_signal(barrier, inc=1, device_id={axis: index(k)}, device_id_type=MESH)
            return carry

        lax.fori_loop(0, count - 1, one, 0)

    greet("blk", blk_index, groups)
    greet("pair", y_index, side)
    greet("pair", z_index, side)

    def send(axis, peer, src, dst, sent, arrived):
        pltpu.make_async_remote_copy(
            src_ref=src, dst_ref=dst, send_sem=sent, recv_sem=arrived,
            device_id={axis: peer}, device_id_type=MESH,
        ).start()

    entries = groups * capacity
    row = lax.broadcasted_iota(jnp.int32, (rows, HALF), 0)
    lane = lax.broadcasted_iota(jnp.int32, (rows, HALF), 1)
    group, member = row // GROUP_ROWS, row % GROUP_ROWS
    listed = member < capacity
    own_lane = jnp.where(listed, group * capacity + member, -1)[:, :entries] == lane[:, :entries]

    def column(values):
        picked = jnp.where(own_lane, values.astype(F32), 0.0)
        total = jnp.sum(picked, axis=1, keepdims=True)
        return jnp.broadcast_to(total, (rows, HALF)).astype(jnp.int32)

    shape_ids = (groups, GROUP_ROWS, HALF)
    source_id = column(pairs_v[0:1, :])
    target_id = column(pairs_v[1:2, :])
    live = listed & (target_id >= 0)
    ids_src[...] = jnp.where(live, source_id - b * nb, -1).reshape(shape_ids)
    table_rows = owner.shape[0]
    high = jnp.where(target_id[:, :table_rows] // HALF == lane[:, :table_rows], 1.0, 0.0)
    slot = gather(high.astype(BF16), split3(owner[...].astype(F32)))
    slot = jnp.sum(jnp.where(target_id % HALF == lane, slot, 0.0), axis=1, keepdims=True)
    slot = jnp.broadcast_to(slot, (rows, HALF)).astype(jnp.int32)
    ids_send[...] = jnp.where(live, slot - group * nb, -1).reshape(shape_ids)

    pl.semaphore_wait(barrier, groups - 1 + 2 * (side - 1))

    def send_ids(k, carry):
        g = blk_index(k)
        send("blk", g, ids_send.at[g], ids_tgt.at[b], ids_sem.at[0], ids_sem.at[1])
        return carry

    lax.fori_loop(0, groups - 1, send_ids, 0)
    ids_tgt[b] = ids_send[b]

    def vector_half(ref, h):
        return ref[pl.ds(h, nb, stride=2), :]

    def pick_matrix(ids, pick):
        ids = ids[...].reshape(rows, HALF)
        wide = jnp.concatenate([ids] * (nb // HALF), axis=1) if nb > HALF else ids[:, :nb]
        match = wide == lax.broadcasted_iota(jnp.int32, (rows, nb), 1)
        pick[...] = jnp.where(match, 1.0, 0.0).astype(BF16)

    lane_row = lane % entries
    lane_place = (lane_row % groups) * GROUP_ROWS + lane_row // groups

    def make_list(ids):
        ids = ids[...].reshape(rows, HALF).astype(F32)
        inside = lane < 3 * entries
        lanes = jnp.sum(jnp.where((row == lane_place) & inside, ids, 0.0), axis=0, keepdims=True)
        before = listed & (member * groups + group < lane_row)
        again = jnp.max(jnp.where((ids == lanes) & before, 1.0, 0.0), axis=0, keepdims=True)
        once = jnp.where((again > 0.0) | jnp.logical_not(inside[0:1, :]), -1.0, lanes)
        line = lax.broadcasted_iota(jnp.int32, (GROUP_ROWS, HALF), 0)
        return jnp.where(line == 0, lanes, jnp.where(line == 1, once, -1.0)).astype(jnp.int32)

    def send_list(s):
        for axis, (index, mine) in enumerate(((y_index, y), (z_index, z))):
            spot = lists.at[s, axis, mine]

            def one(k, carry, index=index, spot=spot, axis=axis):
                sems = list_sem.at[s, axis]
                send("pair", index(k), spot, spot, sems.at[0], sems.at[1])
                return carry

            lax.fori_loop(0, side - 1, one, 0)

    def read_lists(s):
        block = lax.broadcasted_iota(jnp.int32, (nb, HALF), 0)
        lane_nb = lax.broadcasted_iota(jnp.int32, (nb, HALF), 1)
        ones = jnp.ones((HALF, HALF), BF16)
        row_e = lax.broadcasted_iota(jnp.int32, (entries, HALF), 0)
        lane_e = lax.broadcasted_iota(jnp.int32, (entries, HALF), 1)
        for axis in range(2):
            wait_bytes(lists.at[s, axis, pl.ds(0, side - 1)], list_sem.at[s, axis, 1])

            def one(i, carry, axis=axis):
                match = jnp.where(block == lists[s, axis, i, 1:2, :], 1.0, 0.0)
                count = jnp.dot(match.astype(BF16), ones, preferred_element_type=F32)
                none = jnp.where(count > 0.5, 0.0, 1.0)
                place[s, axis, i] = jnp.where(lane_nb == 3 * entries, none, match).astype(BF16)
                return carry

            lax.fori_loop(0, side, one, 0)
            columns = []
            for i in range(side):
                ids = jnp.where(row_e == lane_e, lists[s, axis, i, 0:1, :], 0).astype(F32)
                ids = jnp.sum(ids, axis=1, keepdims=True)
                columns.append(jnp.broadcast_to(ids, (entries, HALF)).astype(jnp.int32))
            ids = jnp.concatenate(columns, axis=0)
            wide = jnp.concatenate([ids] * (nb // HALF), axis=1) if nb > HALF else ids[:, :nb]
            match = wide == lax.broadcasted_iota(jnp.int32, (side * entries, nb), 1)
            pick[s, axis] = jnp.where(match, 1.0, 0.0).astype(BF16)

    def to_compact(ref, target):
        for c in range(capacity):
            for g in range(groups):
                target[c, g : g + 1, :] = ref[g, c : c + 1, :]

    def to_wide(values, target):
        for c in range(capacity):
            for g in range(groups):
                target[g, c : c + 1, :] = values[c, g : g + 1, :]

    row8 = lax.broadcasted_iota(jnp.int32, (GROUP_ROWS, BS), 0)
    row8_half = lax.broadcasted_iota(jnp.int32, (GROUP_ROWS, HALF), 0)

    def pack_rows(points, scale, flipped, bias_row):
        square = points[0] * points[0] + points[1] * points[1] + points[2] * points[2]
        norm = square * (-INV_EPS2)
        lines = [point * scale for point in points]
        lines += [1.0, norm] if flipped else [norm, 1.0]
        lines.append(bias_row)
        packed = jnp.zeros((GROUP_ROWS, BS), F32)
        for r, line in enumerate(lines):
            packed = jnp.where(row8 == r, line, packed)
        return packed

    def own_list(s, ids):
        tile = make_list(ids)
        lists[s, 0, y] = tile
        lists[s, 1, z] = tile
        send_list(s)
        to_compact(ids, own_ids.at[s])

    for i in range(3):
        for j, part in enumerate(split3(tgt_pts[i])):
            table[i, j] = part.astype(BF16)
    for h in range(2):
        first = vector_half(tgt_mass, h) * LOG2E + vector_half(warm, h) * INV_EPS2
        for j, part in enumerate(split3(first)):
            table[3, j, :, lanes_of(h)] = part.astype(BF16)
    low_half = jnp.full(shape_ids, LOW, F32)
    for h in range(2):
        terms[h] = low_half
        partial[h] = low_half
        send_pot[h] = low_half
    shape3 = (groups, GROUP_ROWS, BS)
    own_list(0, ids_src)
    pick_matrix(ids_src, pick_src)
    for i in range(3):
        got_src[i] = gather(pick_src[...], split3(src_pts[i])).reshape(shape3)

    wait_bytes(ids_tgt.at[pl.ds(0, groups - 1)], ids_sem.at[1])
    pick_matrix(ids_tgt, pick_tgt)
    for i in range(4):
        found = gather(pick_tgt[...], [table[i, j] for j in range(3)]).reshape(shape3)
        for g in range(groups):
            got_send[g, i] = found[g]

    def send_pack(k, carry):
        g = blk_index(k)
        send("blk", g, got_send.at[g], got_recv.at[b], pack_sent, pack_sem.at[b])
        return carry

    lax.fori_loop(0, groups - 1, send_pack, 0)
    got_recv[b] = got_send[b]

    def source_group(g, carry):
        for c in range(capacity):
            k = g * capacity + c
            points = [got_src[i, g, c : c + 1, :] for i in range(3)]
            packed = pack_rows(points, 2.0 * INV_EPS2, True, 1.0)
            src_pack[k] = packed
            right_src[k] = right_parts(packed)
        return carry

    lax.fori_loop(0, groups, source_group, 0)
    own_list(1, ids_tgt)
    for h in range(2):
        found = gather(pick_src[...], split3(vector_half(src_mass, h) * LOG2E))
        mass_src[h] = found.reshape(shape_ids)
        found = gather(pick_tgt[...], split3(vector_half(tgt_mass, h) * LOG2E))
        mass_tgt[h] = found.reshape(shape_ids)

    def merge(s, values, target):
        to_compact(values, values_c)

        def one(c, carry):
            for g in range(groups):
                same = own_ids[s].reshape(entries, HALF) == own_ids[s, c, g : g + 1, :]
                picked = jnp.where(same, values_c[...].reshape(entries, HALF), LOW)
                top = jnp.max(picked, axis=0, keepdims=True)
                total = jnp.sum(jnp.exp2(picked - top), axis=0, keepdims=True)
                target[c, g : g + 1, :] = top + log2(total)
            return carry

        lax.fori_loop(0, capacity, one, 0)

    def put(matrix, values):
        one, two, three = split3(values.reshape(entries, HALF))
        none = jnp.full((HALF - 3 * entries, HALF), LOW, F32)
        parts = jnp.concatenate((one, two, three, none), axis=0).astype(BF16)
        return jnp.dot(matrix, parts, preferred_element_type=F32)

    places = (y, z)
    firsts = (y_index, z_index)
    seconds = (z_index, y_index)

    def coordinate(h, peer):
        return lax.rem(peer, side) if h == 0 else peer // side

    def spread_start(a, h):
        mine = places[h]
        sems = spread_sem.at[a, h, 0]

        def one(k, carry):
            send("pair", firsts[h](k), spread.at[a, h], spread_got.at[a, h, mine], sems.at[0], sems.at[1])
            return carry

        lax.fori_loop(0, side - 1, one, 0)
        spread_got[a, h, mine] = spread[a, h]

    def spread_second(a, h, s):
        wait_bytes(spread_got.at[a, h, pl.ds(0, side - 1)], spread_sem.at[a, h, 0, 1])
        for i in range(side):
            placed[i] = put(place[s, h, i], spread_got[a, h, i])
        step = min(nb, 64)
        for q in range(nb // step):
            arrived = placed[:, q * step : (q + 1) * step, :]
            top = jnp.max(arrived, axis=0)
            total = jnp.sum(jnp.exp2(arrived - top[None]), axis=0)
            row_sum[h, q * step : (q + 1) * step, :] = top + log2(total)
        found = gather(pick[s, 1 - h], split3(row_sum[h]))
        asked[a, h] = found.reshape(side, capacity, groups, HALF)
        other = places[1 - h]
        sems = spread_sem.at[a, h, 1]

        def one(k, carry):
            peer = seconds[h](k)
            spot = asked.at[a, h, coordinate(1 - h, peer)]
            send("pair", peer, spot, asked_got.at[a, h, other], sems.at[0], sems.at[1])
            return carry

        lax.fori_loop(0, side - 1, one, 0)
        asked_got[a, h, other] = asked[a, h, other]

    def spread_end(a, h):
        wait_bytes(asked_got.at[a, h, pl.ds(0, side - 1)], spread_sem.at[a, h, 1, 1])
        arrived = asked_got[a, h]
        top = jnp.maximum(jnp.max(arrived, axis=0), 0.0)
        total = jnp.exp2(-top) + jnp.sum(jnp.exp2(arrived - top[None]), axis=0)
        return top + log2(total)

    def own_chunk(h):
        return pl.ds(pl.multiple_of(places[h] * seg, seg), seg)

    def reduce_start(h):
        mine = places[h]

        def one(k, carry):
            peer = firsts[h](k)
            chunk = pl.ds(pl.multiple_of(coordinate(h, peer) * seg, seg), seg)
            sems = red_sem.at[1, h, 0]
            send("pair", peer, dense.at[h, chunk], stage1.at[h, mine], sems.at[0], sems.at[1])
            return carry

        lax.fori_loop(0, side - 1, one, 0)
        stage1[h, mine] = dense[h, own_chunk(h), :]

    def reduce_second(o, h):
        other = places[1 - h]
        if o == 0:
            stage2[o, h, other] = row_sum[h, own_chunk(h), :]
        else:
            wait_bytes(stage1.at[h, pl.ds(0, side - 1)], red_sem.at[o, h, 0, 1])
            arrived = stage1[h]
            top = jnp.max(arrived, axis=0)
            stage2[o, h, other] = top + log2(jnp.sum(jnp.exp2(arrived - top[None]), axis=0))
        sems = red_sem.at[o, h, 1]

        def one(k, carry):
            spot = stage2.at[o, h, other]
            send("pair", seconds[h](k), spot, spot, sems.at[0], sems.at[1])
            return carry

        lax.fori_loop(0, side - 1, one, 0)

    def reduce_third(o, h):
        wait_bytes(stage2.at[o, h, pl.ds(0, side - 1)], red_sem.at[o, h, 1, 1])
        arrived = stage2[o, h]
        top = jnp.maximum(jnp.max(arrived, axis=0), 0.0)
        total = jnp.exp2(-top) + jnp.sum(jnp.exp2(arrived - top[None]), axis=0)
        full[o, h, own_chunk(h), :] = top + log2(total)
        sems = red_sem.at[o, h, 2]

        def one(k, carry):
            spot = full.at[o, h, own_chunk(h)]
            send("pair", firsts[h](k), spot, spot, sems.at[0], sems.at[1])
            return carry

        lax.fori_loop(0, side - 1, one, 0)

    def reduce_end(o, h, out):
        wait_bytes(full.at[o, h, pl.ds(0, (side - 1) * seg)], red_sem.at[o, h, 2, 1])
        out[pl.ds(h, nb, stride=2), :] = full[o, h] * (-EPSILON * LN2)

    def entries_of(gs):
        return [(g, c, g * capacity + c) for g in gs for c in range(capacity)]

    def by_pairs(step, order):
        def one(i, carry):
            step([order(2 * i), order(2 * i + 1)])
            return carry

        lax.fori_loop(0, groups // 2, one, 0)

    def as_they_come(step, ref, sem):
        wait_bytes(ref.at[near(1)], sem.at[near(1)])
        step([near(0), near(1)])

        def one(i, carry):
            gs = [near(2 * i), near(2 * i + 1)]
            for g in gs:
                wait_bytes(ref.at[g], sem.at[g])
            step(gs)
            return carry

        lax.fori_loop(1, groups // 2, one, 0)

    def store_rows(ref, where, totals):
        for (g, c, k), total in zip(where, totals):
            ref[g, c : c + 1, :] = total

    def first_rows(gs):
        where = entries_of(gs)
        packs = []
        for g, c, k in where:
            points = [got_recv[g, i, c : c + 1, :] for i in range(3)]
            packs.append(pack_rows(points, 1.0, False, got_recv[g, 3, c : c + 1, :]))
        lefts = [left_parts(packed) for packed in packs]
        totals = tile_all(lefts, [right_src[k, :, lanes_of(0)] for g, c, k in where])
        for (g, c, k), packed, here in zip(where, packs, lefts):
            tgt_pack[k] = packed
            left[k] = here
        store_rows(terms.at[0], where, totals)

    def second_rows(gs):
        where = entries_of(gs)
        lefts = [left[k] for g, c, k in where]
        store_rows(terms.at[1], where, tile_all(lefts, [right_src[k, :, lanes_of(1)] for g, c, k in where]))

    def row_lefts(h, where):
        return [
            left_parts(
                jnp.where(row8_half == 5, recv_pot[h, g, c : c + 1, :], tgt_pack[k, :, lanes_of(h)])
            )
            for g, c, k in where
        ]

    def store_halves(where, totals):
        for out in range(2):
            store_rows(partial.at[out], where, [total[:, lanes_of(out)] for total in totals])

    def early_rows(gs):
        where = entries_of(gs)
        store_halves(where, tile_all(row_lefts(0, where), [right_src[k] for g, c, k in where]))

    def late_rows(gs):
        where = entries_of(gs)
        lefts = row_lefts(1, where)
        totals = tile_all(lefts, [right_src[k, :, lanes_of(0)] for g, c, k in where])
        for (g, c, k), here in zip(where, lefts):
            left[k, :, lanes_of(1)] = here
        store_rows(terms.at[0], where, totals)

    def last_rows(gs):
        where = entries_of(gs)
        lefts = [left[k, :, lanes_of(1)] for g, c, k in where]
        store_rows(terms.at[1], where, tile_all(lefts, [right_src[k, :, lanes_of(1)] for g, c, k in where]))

    def column_lefts(h, where):
        return [
            left_parts(
                jnp.where(row8_half == 5, bias[h, g, c : c + 1, :], src_pack[k, :, lanes_of(h)])
            )
            for g, c, k in where
        ]

    def early_columns(gs):
        where = entries_of(gs)
        store_halves(where, tile_all(column_lefts(0, where), [right_tgt[k] for g, c, k in where]))

    def late_columns(it, out, gs):
        where = entries_of(gs)
        if out == 0:
            lefts = column_lefts(1, where)
        else:
            lefts = [left[k, :, lanes_of(1)] for g, c, k in where]
        totals = tile_all(lefts, [right_tgt[k, :, lanes_of(out)] for g, c, k in where])
        if out == 0:
            for (g, c, k), here in zip(where, lefts):
                left[k, :, lanes_of(1)] = here
        store_rows(terms.at[out], where, totals)
        for g in gs:
            send_col[it, out, g] = lse_pair(partial[out, g], terms[out, g])

    def target_group(gs):
        for g, c, k in entries_of(gs):
            right_tgt[k] = right_parts(jnp.where(row8 == 5, 1.0, tgt_pack[k]))

    for it in range(ITERS):
        a_src, a_tgt = 2 * it, 2 * it + 1
        last = it == ITERS - 1
        if it == 0:
            as_they_come(first_rows, got_recv, pack_sem)
        else:
            for h in range(2):
                to_wide(spread_end(a_src - 1, h), send_pot.at[h])
                send_pot[h] = mass_tgt[h] - send_pot[h]

                def pot_send(k, carry, h=h):
                    g = blk_index(k)
                    send("blk", g, send_pot.at[h, g], recv_pot.at[h, b], pot_sent.at[h], pot_sem.at[h, b])
                    return carry

                lax.fori_loop(0, groups - 1, pot_send, 0)
                recv_pot[h, b] = send_pot[h, b]
            as_they_come(early_rows, recv_pot.at[0], pot_sem.at[0])
            as_they_come(late_rows, recv_pot.at[1], pot_sem.at[1])
            terms[0] = lse_pair(partial[0], terms[0])
        merge(0, terms.at[0], spread.at[a_src, 0])
        spread_start(a_src, 0)
        by_pairs(second_rows if it == 0 else last_rows, near)
        if it > 0:
            terms[1] = lse_pair(partial[1], terms[1])
        merge(0, terms.at[1], spread.at[a_src, 1])
        spread_start(a_src, 1)
        if it == 0:
            read_lists(0)
        for h in range(2):
            spread_second(a_src, h, 0)
        if last:
            for h in range(2):
                reduce_second(0, h)
        if it == 0:
            by_pairs(target_group, near)
            read_lists(1)
        for h in range(2):
            to_wide(spread_end(a_src, h), bias.at[h])
            bias[h] = mass_src[h] - bias[h]
            if h == 0:
                by_pairs(early_columns, near)
        for out in range(2):
            def send_columns(gs, out=out, it=it):
                late_columns(it, out, gs)
                sems = col_sem.at[it, out]
                for g in gs:
                    send(
                        "blk", g, send_col.at[it, out, g], recv_col.at[it, out, b],
                        sems.at[0], sems.at[1],
                    )

            def far_pair(i, carry, send_columns=send_columns):
                send_columns([blk_index(2 * i), blk_index(2 * i + 1)])
                return carry

            lax.fori_loop(0, groups // 2 - 1, far_pair, 0)
            late_columns(it, out, [near(1), b])
            sems = col_sem.at[it, out]
            send(
                "blk", near(1), send_col.at[it, out, near(1)], recv_col.at[it, out, b],
                sems.at[0], sems.at[1],
            )
            recv_col[it, out, b] = send_col[it, out, b]
        if last:
            for h in range(2):
                reduce_third(0, h)
        for out in range(2):
            wait_bytes(recv_col.at[it, out, pl.ds(0, groups - 1)], col_sem.at[it, out, 1])
            if last:
                merge(1, recv_col.at[it, out], merged)
                dense[out] = put(place[1, 0, y], merged[...])
                reduce_start(out)
            else:
                merge(1, recv_col.at[it, out], spread.at[a_tgt, out])
                spread_start(a_tgt, out)
        if not last:
            for h in range(2):
                spread_second(a_tgt, h, 1)

    for h in range(2):
        reduce_end(0, h, out_src)
    for step in (reduce_second, reduce_third):
        for h in range(2):
            step(1, h)
    for h in range(2):
        reduce_end(1, h, out_tgt)

    def drain(sem, ref, count):
        def one(k, carry):
            wait_bytes(ref, sem)
            return carry

        lax.fori_loop(1, count, one, 0)

    drain(ids_sem.at[0], ids_send.at[0], groups)
    drain(pack_sent, got_send.at[0], groups)
    for h in range(2):
        if ITERS > 1:
            drain(pot_sent.at[h], send_pot.at[h, 0], groups)
        for it in range(ITERS):
            drain(col_sem.at[it, h, 0], send_col.at[it, h, 0], groups)
        for a in range(2 * ITERS - 1):
            for stage in range(2):
                drain(spread_sem.at[a, h, stage, 0], spread.at[a, h], side)
        for o in range(2):
            for stage in range(1 - o, 3):
                drain(red_sem.at[o, h, stage, 0], dense.at[h, pl.ds(0, seg)], side)
        for s in range(2):
            drain(list_sem.at[s, h, 0], lists.at[s, h, 0], side)


def per_device(
    source_points, target_points, source_logw, target_logw, warm_start, pairs, owner_slot
):
    groups = lax.axis_size("blk")
    side = round(lax.axis_size("pair") ** 0.5)
    points = source_logw.shape[0]
    nb = points // BS
    capacity = pairs.shape[-1] // groups
    entries = groups * capacity
    rows = groups * GROUP_ROWS
    seg = nb // side
    reductions = 2 * ITERS - 1
    slots = -(-owner_slot.shape[0] // 2048) * 2048
    owner = jnp.pad(owner_slot, (0, slots - owner_slot.shape[0])).reshape(-1, HALF)
    vmem = pl.BlockSpec(memory_space=pltpu.VMEM)
    out = jax.ShapeDtypeStruct((points // HALF, HALF), F32)
    dma = pltpu.SemaphoreType.DMA
    tall = 6 * GROUP_ROWS
    source_pot, target_pot = pl.pallas_call(
        functools.partial(kernel, groups, side, capacity, nb),
        out_shape=(out, out),
        in_specs=[vmem] * 7,
        out_specs=(vmem, vmem),
        scratch_shapes=[
            *[pltpu.VMEM((groups, GROUP_ROWS, HALF), jnp.int32)] * 3,
            pltpu.VMEM((2, capacity, groups, HALF), jnp.int32),
            pltpu.VMEM((2, 2, side, GROUP_ROWS, HALF), jnp.int32),
            pltpu.VMEM((2, 2, side, nb, HALF), BF16),
            pltpu.VMEM((2, 2, side * entries, nb), BF16),
            *[pltpu.VMEM((rows, nb), BF16)] * 2,
            pltpu.VMEM((4, 3, nb, BS), BF16),
            pltpu.VMEM((3, groups, GROUP_ROWS, BS), F32),
            *[pltpu.VMEM((groups, 4, GROUP_ROWS, BS), F32)] * 2,
            *[pltpu.VMEM((entries, GROUP_ROWS, BS), F32)] * 2,
            *[pltpu.VMEM((entries, tall, BS), BF16)] * 3,
            *[pltpu.VMEM((2, groups, GROUP_ROWS, HALF), F32)] * 7,
            *[pltpu.VMEM((capacity, groups, HALF), F32)] * 2,
            *[pltpu.VMEM((ITERS, 2, groups, GROUP_ROWS, HALF), F32)] * 2,
            pltpu.VMEM((reductions, 2, capacity, groups, HALF), F32),
            pltpu.VMEM((reductions, 2, side, capacity, groups, HALF), F32),
            pltpu.VMEM((side, nb, HALF), F32),
            pltpu.VMEM((2, nb, HALF), F32),
            *[pltpu.VMEM((reductions, 2, side, capacity, groups, HALF), F32)] * 2,
            pltpu.VMEM((2, nb, HALF), F32),
            pltpu.VMEM((2, side, seg, HALF), F32),
            pltpu.VMEM((2, 2, side, seg, HALF), F32),
            pltpu.VMEM((2, 2, nb, HALF), F32),
            dma((2,)),
            dma((2, 2, 2)),
            dma,
            dma((groups,)),
            dma((2,)),
            dma((2, groups)),
            dma((ITERS, 2, 2)),
            dma((reductions, 2, 2, 2)),
            dma((2, 2, 3, 2)),
        ],
        compiler_params=pltpu.CompilerParams(
            collective_id=0, has_side_effects=True, vmem_limit_bytes=40 * 1024 * 1024
        ),
        name="sinkhorn",
    )(
        pairs[0, 0], owner,
        source_points.reshape(3, nb, BS), target_points.reshape(3, nb, BS),
        source_logw.reshape(-1, HALF), target_logw.reshape(-1, HALF), warm_start.reshape(-1, HALF),
    )
    return source_pot.reshape(-1), target_pot.reshape(-1)


def solution(mesh):
    return jax.shard_map(
        per_device,
        mesh=mesh,
        in_specs=(
            P(None, "blk"),
            P(None, "blk"),
            P("blk"),
            P("blk"),
            P("blk"),
            P("blk", "pair", None, None),
            P(),
        ),
        out_specs=(P("blk"), P("blk")),
        check_vma=False,
    )
```

time: 1360 us -> 110 us (0.08)
  waiting for transfers between devices: 1170 us -> 0 us
  Pallas kernels: 0 us -> 105 us
  other arithmetic: 99.5 us -> 0 us
  starting transfers between devices: 29.8 us -> 0 us
  blocking collectives: 18.9 us -> 0 us
  between operations: 14.6 us -> 0.71 us
    psum x4 -> x0, waiting for transfers between devices: 599 us -> none  [pair_combine(): total = lax.psum(block_sum * jnp.exp(block_max - top), 'pair')]
    pmax x4 -> x0, waiting for transfers between devices: 560 us -> none  [pair_combine(): top = lax.pmax(block_max, 'pair')]
    pallas_call x0 -> x1, Pallas kernels: none -> 105 us  [per_device(): pl.pallas_call(functools.partial(kernel, groups, side, capacity, nb), out...]
    reduce_max x8 -> x0, other arithmetic: 47.4 us -> none  [the longest x4 17.1 us: collect(): jnp.max(jnp.where(onehot[:, :, None], slot_max[None], VERY_LOW), axis=1)]
    reduce_sum x4 -> x0, other arithmetic: 35.9 us -> none  [the longest x2 18.5 us: per_device(): row_sum = jnp.sum(jnp.exp(row_term - row_max[:, :, None]), axis=2)]
    all_to_all x5 -> x0, starting transfers between devices: 29.4 us -> none  [the longest x2 10.7 us: per_device(): lax.all_to_all(col_sum.reshape(groups, capacity, block_size), 'blk', spli...]
    all_to_all x2 -> x0, blocking collectives: 18.9 us -> none  [the longest x1 10.8 us: per_device(): lax.all_to_all(whole_pack, 'blk', split_axis=1, concat_axis=1, tiled=True)]
  transfers between devices with their start and end apart: 13 -> 0, of which waited for: 12 -> 0; matrix products, arithmetic and copies ran while one was open for 2% -> 0% of each run, Pallas kernels for 0% -> 0%
where the time goes in v2:
time: 110 us; the launch traced here: 109 us
  Pallas kernels  105 us (95%)
  local copies, waits for them, and re-layouts  4 us (4%)
    pallas_call x1, Pallas kernels, per_device(): pl.pallas_call(functools.partial(kernel, groups, side, capacity, nb), out...  105 us

profile of v2, /device:TPU:6, one launch (start us, length us, event | category | flops | bytes accessed | tf_op | source)
XLA Modules:
  0.0 109.5 jit_solution(4239267863211189527)
XLA Ops:
  0.6 0.0 copy-start
  0.6 0.0 copy-start.1
  0.7 0.0 copy-start.2
  0.7 0.0 copy-start.3
  0.7 1.9 %copy_bitcast_fusion = (f32[3,256,256]{2,1,0:T(8,128)S(1)}, f32[3,256,256]{2,1,0:T(8,128)S(1)}) fusion(f32[1,3,256,256]{3,1,2,0:T(4,128)} %bitcast.20, f32[1,3,256,256]{3,1,2,0:T(4,128)} %bitcast.21), kind=kLoop, calls=%fused_computation | loop fusion | bytes 3145728 | tf_op jit(solution)/shard_map/reshape | solution.py:705
  2.6 0.0 copy-start.4
  2.6 0.0 copy-done
  2.6 0.0 copy-done.1
  2.6 0.0 copy-done.2
  2.6 0.0 copy-done.3
  2.6 0.6 copy-done.4
  3.3 104.7 %sinkhorn.1 = (f32[512,128]{1,0:T(8,128)S(1)}, f32[512,128]{1,0:T(8,128)S(1)}) custom-call(s32[2,40]{1,0:T(2,128)S(1)} %bitcast.19, s32[16,128]{1,0:T(8,128)S(1)} %bitcast.18, f32[3,256,256]{2,1,0:T(8,128)S(1)} %get-tuple-element.7.src_pts, f32[3,256,256]{2,1,0:T(8,128)S(1)} %get-tuple-element.6.tgt_pts, f32[512,128]{1,0:T(8,128)S(1)} %bitcast.13, ...), custom_call_target="tpu_custom_call" | custom-call | tf_op jit(solution)/shard_map/sinkhorn/pallas_call | solution.py:660
  108.0 0.7 copy.15
  108.7 0.7 copy.16
Async XLA Ops:
  0.6 2.0 %copy-start = (f32[65536]{0:T(1024)S(1)}, f32[65536]{0:T(1024)}, u32[]{:S(2)}) copy-start(f32[65536]{0:T(1024)} %param.9) | copy-start | bytes 786436
  0.6 2.0 %copy-start.1 = (f32[65536]{0:T(1024)S(1)}, f32[65536]{0:T(1024)}, u32[]{:S(2)}) copy-start(f32[65536]{0:T(1024)} %param.10) | copy-start | bytes 786436
  0.7 2.0 %copy-start.2 = (f32[65536]{0:T(1024)S(1)}, f32[65536]{0:T(1024)}, u32[]{:S(2)}) copy-start(f32[65536]{0:T(1024)} %param.11) | copy-start | bytes 786436
  0.7 2.0 %copy-start.3 = (s32[2048]{0:T(1024)S(1)}, s32[2048]{0:T(1024)}, u32[]{:S(2)}) copy-start(s32[2048]{0:T(1024)} %param.13) | copy-start | bytes 24580
  2.6 0.7 copy-start.4

commit v3 on v2

--- a/solution.py
+++ b/solution.py
@@ -10,6 +10,7 @@
 BS = 256
 HALF = 128
 ITERS = 2
+BATCH = 4
 GROUP_ROWS = 8
 LOG2E = 1.4426950408889634
 LN2 = 0.6931471805599453
@@ -79,8 +80,16 @@
 
 def kernel(
     groups, side, capacity, nb,
-    pairs_v, owner, src_pts, tgt_pts, src_mass, tgt_mass, warm,
-    out_src, out_tgt,
+    pairs_v, owner, *operands_and_rest,
+):
+    inputs, rest = operands_and_rest[:5], operands_and_rest[5:]
+    held, rest = rest[2:7], rest[:2] + rest[7:]
+    run(groups, side, capacity, nb, pairs_v, owner, inputs, held, *rest)
+
+
+def run(
+    groups, side, capacity, nb, pairs_v, owner, inputs, held,
+    out_src, out_tgt, src_blocks, tgt_blocks, input_sem,
     ids_send, ids_src, ids_tgt, own_ids, lists, place, pick, pick_src, pick_tgt, table,
     got_src, got_send, got_recv, src_pack, tgt_pack, left, right_src, right_tgt,
     mass_src, mass_tgt, bias, send_pot, recv_pot, terms, partial, values_c, merged, send_col, recv_col,
@@ -107,6 +116,12 @@
     def z_index(k):
         return lax.rem(z + far_first(k, side), side) * side + y
 
+    copies = []
+    for i, (outside, inside) in enumerate(zip(inputs, held)):
+        copies.append(pltpu.make_async_copy(outside, inside, input_sem.at[i]))
+        copies[i].start()
+    tgt_pts, tgt_mass, warm, src_pts, src_mass = held
+
     barrier = pltpu.get_barrier_semaphore()
 
     def greet(axis, index, count):
@@ -150,6 +165,32 @@
     slot = jnp.broadcast_to(slot, (rows, HALF)).astype(jnp.int32)
     ids_send[...] = jnp.where(live, slot - group * nb, -1).reshape(shape_ids)
 
+    def by_blocks(points, blocks):
+        def eight(q, carry):
+            for r in range(GROUP_ROWS):
+                first = pl.multiple_of((q * GROUP_ROWS + r) * BS, BS)
+                value = points[:, pl.ds(first, BS)]
+                for i in range(3):
+                    blocks[i, q, r : r + 1, :] = value[i : i + 1, :]
+            return carry
+
+        lax.fori_loop(0, nb // GROUP_ROWS, eight, 0)
+
+    def vector_half(ref, h):
+        return ref[pl.ds(h, nb, stride=2), :]
+
+    copies[0].wait()
+    by_blocks(tgt_pts, tgt_blocks)
+    for i in range(3):
+        for j, part in enumerate(split3(tgt_blocks[i].reshape(nb, BS))):
+            table[i, j] = part.astype(BF16)
+    copies[1].wait()
+    copies[2].wait()
+    for h in range(2):
+        first = vector_half(tgt_mass, h) * LOG2E + vector_half(warm, h) * INV_EPS2
+        for j, part in enumerate(split3(first)):
+            table[3, j, :, lanes_of(h)] = part.astype(BF16)
+
     pl.semaphore_wait(barrier, groups - 1 + 2 * (side - 1))
 
     def send_ids(k, carry):
@@ -159,9 +200,6 @@
 
     lax.fori_loop(0, groups - 1, send_ids, 0)
     ids_tgt[b] = ids_send[b]
-
-    def vector_half(ref, h):
-        return ref[pl.ds(h, nb, stride=2), :]
 
     def pick_matrix(ids, pick):
         ids = ids[...].reshape(rows, HALF)
@@ -251,13 +289,6 @@
         send_list(s)
         to_compact(ids, own_ids.at[s])
 
-    for i in range(3):
-        for j, part in enumerate(split3(tgt_pts[i])):
-            table[i, j] = part.astype(BF16)
-    for h in range(2):
-        first = vector_half(tgt_mass, h) * LOG2E + vector_half(warm, h) * INV_EPS2
-        for j, part in enumerate(split3(first)):
-            table[3, j, :, lanes_of(h)] = part.astype(BF16)
     low_half = jnp.full(shape_ids, LOW, F32)
     for h in range(2):
         terms[h] = low_half
@@ -266,8 +297,12 @@
     shape3 = (groups, GROUP_ROWS, BS)
     own_list(0, ids_src)
     pick_matrix(ids_src, pick_src)
+    copies[3].wait()
+    copies[4].wait()
+    by_blocks(src_pts, src_blocks)
     for i in range(3):
-        got_src[i] = gather(pick_src[...], split3(src_pts[i])).reshape(shape3)
+        points = src_blocks[i].reshape(nb, BS)
+        got_src[i] = gather(pick_src[...], split3(points)).reshape(shape3)
 
     wait_bytes(ids_tgt.at[pl.ds(0, groups - 1)], ids_sem.at[1])
     pick_matrix(ids_tgt, pick_tgt)
@@ -304,16 +339,13 @@
     def merge(s, values, target):
         to_compact(values, values_c)
 
-        def one(c, carry):
+        for c in range(capacity):
             for g in range(groups):
                 same = own_ids[s].reshape(entries, HALF) == own_ids[s, c, g : g + 1, :]
                 picked = jnp.where(same, values_c[...].reshape(entries, HALF), LOW)
                 top = jnp.max(picked, axis=0, keepdims=True)
                 total = jnp.sum(jnp.exp2(picked - top), axis=0, keepdims=True)
                 target[c, g : g + 1, :] = top + log2(total)
-            return carry
-
-        lax.fori_loop(0, capacity, one, 0)
 
     def put(matrix, values):
         one, two, three = split3(values.reshape(entries, HALF))
@@ -426,25 +458,28 @@
     def entries_of(gs):
         return [(g, c, g * capacity + c) for g in gs for c in range(capacity)]
 
-    def by_pairs(step, order):
+    def in_batches(step, size):
         def one(i, carry):
-            step([order(2 * i), order(2 * i + 1)])
-            return carry
-
-        lax.fori_loop(0, groups // 2, one, 0)
-
-    def as_they_come(step, ref, sem):
-        wait_bytes(ref.at[near(1)], sem.at[near(1)])
-        step([near(0), near(1)])
-
-        def one(i, carry):
-            gs = [near(2 * i), near(2 * i + 1)]
-            for g in gs:
+            step([near(size * i + j) for j in range(size)])
+            return carry
+
+        lax.fori_loop(0, groups // size, one, 0)
+
+    def as_they_come(step, ref, sem, size):
+        def batch(i, first):
+            gs = [near(size * i + j) for j in range(size)]
+            for g in gs[first:]:
                 wait_bytes(ref.at[g], sem.at[g])
             step(gs)
-            return carry
-
-        lax.fori_loop(1, groups // 2, one, 0)
+
+        def one(i, carry):
+            batch(i, 0)
+            return carry
+
+        batch(0, 1)
+        lax.fori_loop(1, groups // size, one, 0)
+
+    many = min(BATCH, groups)
 
     def store_rows(ref, where, totals):
         for (g, c, k), total in zip(where, totals):
@@ -531,7 +566,7 @@
         a_src, a_tgt = 2 * it, 2 * it + 1
         last = it == ITERS - 1
         if it == 0:
-            as_they_come(first_rows, got_recv, pack_sem)
+            as_they_come(first_rows, got_recv, pack_sem, 2)
         else:
             for h in range(2):
                 to_wide(spread_end(a_src - 1, h), send_pot.at[h])
@@ -544,12 +579,12 @@
 
                 lax.fori_loop(0, groups - 1, pot_send, 0)
                 recv_pot[h, b] = send_pot[h, b]
-            as_they_come(early_rows, recv_pot.at[0], pot_sem.at[0])
-            as_they_come(late_rows, recv_pot.at[1], pot_sem.at[1])
+            as_they_come(early_rows, recv_pot.at[0], pot_sem.at[0], many)
+            as_they_come(late_rows, recv_pot.at[1], pot_sem.at[1], many)
             terms[0] = lse_pair(partial[0], terms[0])
         merge(0, terms.at[0], spread.at[a_src, 0])
         spread_start(a_src, 0)
-        by_pairs(second_rows if it == 0 else last_rows, near)
+        in_batches(second_rows if it == 0 else last_rows, many)
         if it > 0:
             terms[1] = lse_pair(partial[1], terms[1])
         merge(0, terms.at[1], spread.at[a_src, 1])
@@ -562,34 +597,29 @@
             for h in range(2):
                 reduce_second(0, h)
         if it == 0:
-            by_pairs(target_group, near)
+            in_batches(target_group, 2)
             read_lists(1)
         for h in range(2):
             to_wide(spread_end(a_src, h), bias.at[h])
             bias[h] = mass_src[h] - bias[h]
             if h == 0:
-                by_pairs(early_columns, near)
+                in_batches(early_columns, many)
         for out in range(2):
-            def send_columns(gs, out=out, it=it):
+            def send_columns(gs, count, out=out, it=it):
                 late_columns(it, out, gs)
                 sems = col_sem.at[it, out]
-                for g in gs:
+                for g in gs[:count]:
                     send(
                         "blk", g, send_col.at[it, out, g], recv_col.at[it, out, b],
                         sems.at[0], sems.at[1],
                     )
 
-            def far_pair(i, carry, send_columns=send_columns):
-                send_columns([blk_index(2 * i), blk_index(2 * i + 1)])
+            def far_batch(i, carry, send_columns=send_columns):
+                send_columns([blk_index(many * i + j) for j in range(many)], many)
                 return carry
 
-            lax.fori_loop(0, groups // 2 - 1, far_pair, 0)
-            late_columns(it, out, [near(1), b])
-            sems = col_sem.at[it, out]
-            send(
-                "blk", near(1), send_col.at[it, out, near(1)], recv_col.at[it, out, b],
-                sems.at[0], sems.at[1],
-            )
+            lax.fori_loop(0, groups // many - 1, far_batch, 0)
+            send_columns([near(many - 1 - j) for j in range(many)], many - 1)
             recv_col[it, out, b] = send_col[it, out, b]
         if last:
             for h in range(2):
@@ -612,31 +642,31 @@
     for step in (reduce_second, reduce_third):
         for h in range(2):
             step(1, h)
+    def drain(sem, ref):
+        wait_bytes(ref, sem)
+
+    others = pl.ds(0, groups - 1)
+    peers = pl.ds(0, side - 1)
+    drain(ids_sem.at[0], ids_tgt.at[others])
+    drain(pack_sent, got_recv.at[others])
+    for h in range(2):
+        if ITERS > 1:
+            drain(pot_sent.at[h], recv_pot.at[h, others])
+        for it in range(ITERS):
+            drain(col_sem.at[it, h, 0], recv_col.at[it, h, others])
+        for a in range(2 * ITERS - 1):
+            for stage in range(2):
+                drain(spread_sem.at[a, h, stage, 0], spread_got.at[a, h, peers])
+        drain(red_sem.at[1, h, 0, 0], stage1.at[h, peers])
+        for o in range(2):
+            drain(red_sem.at[o, h, 1, 0], stage2.at[o, h, peers])
+        drain(red_sem.at[0, h, 2, 0], stage1.at[h, peers])
+        for s in range(2):
+            drain(list_sem.at[s, h, 0], lists.at[s, h, peers])
     for h in range(2):
         reduce_end(1, h, out_tgt)
-
-    def drain(sem, ref, count):
-        def one(k, carry):
-            wait_bytes(ref, sem)
-            return carry
-
-        lax.fori_loop(1, count, one, 0)
-
-    drain(ids_sem.at[0], ids_send.at[0], groups)
-    drain(pack_sent, got_send.at[0], groups)
     for h in range(2):
-        if ITERS > 1:
-            drain(pot_sent.at[h], send_pot.at[h, 0], groups)
-        for it in range(ITERS):
-            drain(col_sem.at[it, h, 0], send_col.at[it, h, 0], groups)
-        for a in range(2 * ITERS - 1):
-            for stage in range(2):
-                drain(spread_sem.at[a, h, stage, 0], spread.at[a, h], side)
-        for o in range(2):
-            for stage in range(1 - o, 3):
-                drain(red_sem.at[o, h, stage, 0], dense.at[h, pl.ds(0, seg)], side)
-        for s in range(2):
-            drain(list_sem.at[s, h, 0], lists.at[s, h, 0], side)
+        drain(red_sem.at[1, h, 2, 0], stage1.at[h, peers])
 
 
 def per_device(
@@ -660,9 +690,15 @@
     source_pot, target_pot = pl.pallas_call(
         functools.partial(kernel, groups, side, capacity, nb),
         out_shape=(out, out),
-        in_specs=[vmem] * 7,
+        in_specs=[vmem] * 2 + [pl.BlockSpec(memory_space=pl.ANY)] * 5,
         out_specs=(vmem, vmem),
         scratch_shapes=[
+            pltpu.VMEM((3, points), F32),
+            *[pltpu.VMEM((points // HALF, HALF), F32)] * 2,
+            pltpu.VMEM((3, points), F32),
+            pltpu.VMEM((points // HALF, HALF), F32),
+            *[pltpu.VMEM((3, nb // GROUP_ROWS, GROUP_ROWS, BS), F32)] * 2,
+            dma((5,)),
             *[pltpu.VMEM((groups, GROUP_ROWS, HALF), jnp.int32)] * 3,
             pltpu.VMEM((2, capacity, groups, HALF), jnp.int32),
             pltpu.VMEM((2, 2, side, GROUP_ROWS, HALF), jnp.int32),
@@ -697,13 +733,13 @@
             dma((2, 2, 3, 2)),
         ],
         compiler_params=pltpu.CompilerParams(
-            collective_id=0, has_side_effects=True, vmem_limit_bytes=40 * 1024 * 1024
+            collective_id=0, has_side_effects=True, vmem_limit_bytes=56832 * 1024
         ),
         name="sinkhorn",
     )(
         pairs[0, 0], owner,
-        source_points.reshape(3, nb, BS), target_points.reshape(3, nb, BS),
-        source_logw.reshape(-1, HALF), target_logw.reshape(-1, HALF), warm_start.reshape(-1, HALF),
+        target_points, target_logw.reshape(-1, HALF), warm_start.reshape(-1, HALF),
+        source_points, source_logw.reshape(-1, HALF),
     )
     return source_pot.reshape(-1), target_pot.reshape(-1)
 

time: 110 us -> 105 us (0.955)
  Pallas kernels: 105 us -> 102 us
  local copies, waits for them, and re-layouts: 4 us -> 2.44 us
    pallas_call x1, Pallas kernels: 105 us -> 102 us  [per_device(): pl.pallas_call(functools.partial(kernel, groups, side, capacity, nb), out...]
    reshape x1 -> x0, local copies, waits for them, and re-layouts: 1.91 us -> none  [per_device(): target_points.reshape(3, nb, BS)]
    unnamed x12 -> x4, local copies, waits for them, and re-layouts: 2.09 us -> 2.44 us
where the time goes in v3:
time: 105 us
  Pallas kernels  102 us (97%)
  local copies, waits for them, and re-layouts  2.44 us (2%)
    pallas_call x1, Pallas kernels, per_device(): pl.pallas_call(functools.partial(kernel, groups, side, capacity, nb), out...  102 us
    unnamed x4, local copies, waits for them, and re-layouts  2.44 us

profile of v3, /device:TPU:6, one launch (start us, length us, event | category | flops | bytes accessed | tf_op | source)
XLA Modules:
  0.0 104.6 jit_solution(3185445613400530868)
XLA Ops:
  0.6 101.5 %sinkhorn.1 = (f32[512,128]{1,0:T(8,128)}, f32[512,128]{1,0:T(8,128)}) custom-call(s32[2,40]{1,0:T(2,128)} %bitcast.13, s32[16,128]{1,0:T(8,128)} %bitcast.12, f32[3,65536]{1,0:T(4,128)} %operands_and_rest_0_.1, f32[512,128]{1,0:T(8,128)} %bitcast.9, f32[512,128]{1,0:T(8,128)} %bitcast.10, f32[3,65536]{1,0:T(4,128)} %operands_and_rest_3_.1, f32[512,128]{1,0:T(8,128)} %bitcast.11), custom_call_target="tpu_custom_call" | custom-call | tf_op jit(solution)/shard_map/sinkhorn/pallas_call | solution.py:690
  102.2 0.0 copy-start
  102.2 1.7 %copy.11 = f32[65536]{0:T(1024)} copy(f32[65536]{0:T(1024)} %bitcast.8) | data formatting | bytes 524288
  103.9 0.0 copy-done
  103.9 0.7 copy.12
Async XLA Ops:
  102.2 1.7 %copy-start = (f32[512,128]{1,0:T(8,128)S(1)}, f32[512,128]{1,0:T(8,128)}, u32[]{:S(2)}) copy-start(f32[512,128]{1,0:T(8,128)} %get-tuple-element.5) | copy-start | bytes 786436

commit v4 on v3

--- a/solution.py
+++ b/solution.py
@@ -557,6 +557,14 @@
         store_rows(terms.at[out], where, totals)
         for g in gs:
             send_col[it, out, g] = lse_pair(partial[out, g], terms[out, g])
+
+    def all_columns(it, gs):
+        where = entries_of(gs)
+        totals = tile_all(column_lefts(1, where), [right_tgt[k] for g, c, k in where])
+        for out in range(2):
+            store_rows(terms.at[out], where, [total[:, lanes_of(out)] for total in totals])
+            for g in gs:
+                send_col[it, out, g] = lse_pair(partial[out, g], terms[out, g])
 
     def target_group(gs):
         for g, c, k in entries_of(gs):
@@ -604,15 +612,19 @@
             bias[h] = mass_src[h] - bias[h]
             if h == 0:
                 in_batches(early_columns, many)
-        for out in range(2):
-            def send_columns(gs, count, out=out, it=it):
-                late_columns(it, out, gs)
-                sems = col_sem.at[it, out]
-                for g in gs[:count]:
-                    send(
-                        "blk", g, send_col.at[it, out, g], recv_col.at[it, out, b],
-                        sems.at[0], sems.at[1],
-                    )
+        for outs in ((0, 1),) if last else ((0,), (1,)):
+            def send_columns(gs, count, outs=outs, it=it):
+                if len(outs) == 2:
+                    all_columns(it, gs)
+                else:
+                    late_columns(it, outs[0], gs)
+                for out in outs:
+                    sems = col_sem.at[it, out]
+                    for g in gs[:count]:
+                        send(
+                            "blk", g, send_col.at[it, out, g], recv_col.at[it, out, b],
+                            sems.at[0], sems.at[1],
+                        )
 
             def far_batch(i, carry, send_columns=send_columns):
                 send_columns([blk_index(many * i + j) for j in range(many)], many)
@@ -620,7 +632,8 @@
 
             lax.fori_loop(0, groups // many - 1, far_batch, 0)
             send_columns([near(many - 1 - j) for j in range(many)], many - 1)
-            recv_col[it, out, b] = send_col[it, out, b]
+            for out in outs:
+                recv_col[it, out, b] = send_col[it, out, b]
         if last:
             for h in range(2):
                 reduce_third(0, h)
@@ -733,13 +746,18 @@
             dma((2, 2, 3, 2)),
         ],
         compiler_params=pltpu.CompilerParams(
-            collective_id=0, has_side_effects=True, vmem_limit_bytes=56832 * 1024
+            collective_id=0, has_side_effects=True, vmem_limit_bytes=40 * 1024 * 1024
         ),
         name="sinkhorn",
     )(
         pairs[0, 0], owner,
-        target_points, target_logw.reshape(-1, HALF), warm_start.reshape(-1, HALF),
-        source_points, source_logw.reshape(-1, HALF),
+        *[
+            pltpu.with_memory_space_constraint(value, pltpu.HBM)
+            for value in (
+                target_points, target_logw.reshape(-1, HALF), warm_start.reshape(-1, HALF),
+                source_points, source_logw.reshape(-1, HALF),
+            )
+        ],
     )
     return source_pot.reshape(-1), target_pot.reshape(-1)
 

time: 105 us -> 104 us (level)
    unnamed x4 -> x6, local copies, waits for them, and re-layouts: 2.44 us -> 2.12 us
where the time goes in v4:
time: 104 us; the launch traced here: 103 us
  Pallas kernels  101 us (97%)
  local copies, waits for them, and re-layouts  2.12 us (2%)
    pallas_call x1, Pallas kernels, per_device(): pl.pallas_call(functools.partial(kernel, groups, side, capacity, nb), out...  101 us
    unnamed x6, local copies, waits for them, and re-layouts  2.12 us

profile of v4, /device:TPU:6, one launch (start us, length us, event | category | flops | bytes accessed | tf_op | source)
XLA Modules:
  0.0 103.3 jit_solution(3843161339829941047)
XLA Ops:
  0.6 0.0 copy-start
  0.6 0.0 copy-start.1
  0.7 0.7 copy-done
  1.3 0.0 copy-done.1
  1.3 100.5 %sinkhorn.1 = (f32[512,128]{1,0:T(8,128)S(1)}, f32[512,128]{1,0:T(8,128)S(1)}) custom-call(s32[2,40]{1,0:T(2,128)S(1)} %bitcast.10, s32[16,128]{1,0:T(8,128)S(1)} %bitcast.9, f32[3,65536]{1,0:T(4,128)} %operands_and_rest_0_.1, f32[512,128]{1,0:T(8,128)} %bitcast.11, f32[512,128]{1,0:T(8,128)} %bitcast.12, f32[3,65536]{1,0:T(4,128)} %operands_and_rest_3_.1, ...), custom_call_target="tpu_custom_call" | custom-call | tf_op jit(solution)/shard_map/sinkhorn/pallas_call | solution.py:703
  101.9 0.7 copy.11
  102.6 0.7 copy.12
Async XLA Ops:
  0.6 0.7 copy-start
  0.6 0.7 copy-start.1
